TPU v7x, 512 devices: a whole 4x8x8 slice. The times are simulated.
512 devices in a mesh: ia: 16 (over z_lo, x, core), ja: 8 (over y), ka: 4 (over z_hi).
Axes of the slice: x: 4, y: 8, z: 8 (z_hi: 4, z_lo: 2; z = z_hi * 2 + z_lo), core: 2. Of those that a mesh axis runs over, the one named last changes fastest.
Arguments:
- tensor: float32 [512, 1024, 512], P('ia', 'ja', 'ka'), may hold values from -200 to 200
- factor_b: float32 [1024, 4, 96], P(('ja', 'ka')), may hold values from -4 to 4
- factor_c: float32 [512, 4, 96], P(('ka', 'ja')), may hold values from -4 to 4
Outputs:
- factor_a: float32 [512, 4, 96], P(('ia', 'ja', 'ka'))
- weights: float32 [4, 96], replicated
All inputs are finite; a program needn't handle non-finite values.
Results may differ from a plain program's by a relative error of at most 0.0003.
Values sent between devices are 32-bit elements; how exact they have to be, the bound alone decides.
No kernel may reach another device: no remote copies, remote signals or barrier semaphores. Data moves between devices by JAX's collectives and lax.ppermute only.
A program may use at most 64 MiB of HBM per device.

v0:
```python
import jax
import jax.numpy as jnp
from jax import lax
from jax.sharding import PartitionSpec as P

highest = lax.Precision.HIGHEST


def gram_of(rows):
    return jnp.einsum(
        "jsr,jsq->srq", rows, rows, precision=highest, preferred_element_type=jnp.float32
    )


def solve_normal(rows, gram_b, gram_c):
    columns = []
    for member in range(rows.shape[1]):
        normal_mat = gram_b[member] * gram_c[member]
        factor_l = jnp.linalg.cholesky(normal_mat)
        right_side = rows[:, member, :].T
        lower_sol = lax.linalg.triangular_solve(factor_l, right_side, left_side=True, lower=True)
        upper_sol = lax.linalg.triangular_solve(
            factor_l, lower_sol, left_side=True, lower=True, transpose_a=True
        )
        columns.append(upper_sol.T)
    return jnp.stack(columns, axis=1)


def shards(tensor, factor_b, factor_c):
    rows_i, rows_j, rows_k = tensor.shape
    starts, col_count = (factor_b.shape[1], factor_b.shape[2])
    width = starts * col_count
    c_block = lax.all_gather(factor_c, "ja", axis=0, tiled=True)
    partial_value = jnp.dot(
        tensor.reshape(rows_i * rows_j, rows_k),
        c_block.reshape(rows_k, width),
        precision=highest,
        preferred_element_type=jnp.float32,
    ).reshape(rows_i, rows_j, width)
    piece = lax.all_gather(factor_b, "ka", axis=0, tiled=True)
    gram_sum = jnp.zeros((starts, col_count, col_count), jnp.float32)
    count = piece.shape[0]
    flat_rows = piece.reshape(count, width)
    mttkrp = jnp.einsum(
        "ijr,jr->ir",
        partial_value,
        flat_rows,
        precision=highest,
        preferred_element_type=jnp.float32,
    )
    mttkrp, gram_rows = (mttkrp, gram_sum)
    gram_b, gram_c = lax.psum((gram_of(factor_b), gram_of(factor_c)), ("ja", "ka"))
    slab_rows = lax.psum_scatter(mttkrp, "ja", scatter_dimension=0, tiled=True)
    owned = lax.psum_scatter(slab_rows, "ka", scatter_dimension=0, tiled=True)
    owned = owned.reshape(owned.shape[0], starts, col_count)
    factor_raw = solve_normal(owned, gram_b, gram_c)
    squares = jnp.sum(factor_raw * factor_raw, axis=0)
    total = lax.psum(squares, ("ia", "ja", "ka"))
    row_total = rows_i * lax.axis_size("ia")
    weights = jnp.sqrt(total / row_total + 1e-06)
    return (factor_raw / weights[None], weights)


def solution(mesh):
    in_specs = (P("ia", "ja", "ka"), P(("ja", "ka"), None, None), P(("ka", "ja"), None, None))
    out_specs = (P(("ia", "ja", "ka"), None, None), P())
    return jax.shard_map(shards, mesh=mesh, in_specs=in_specs, out_specs=out_specs, check_vma=False)
```

profile of v0, /device:TPU:1, one launch (start us, length us, event | category | flops | bytes accessed | tf_op | source)
XLA Modules:
  0.0 503.4 jit_solution(228719153162087754)
XLA Ops:
  7.2 2.1 fusion.22
  9.3 2.1 fusion
  11.4 18.7 %all_gather.7 = f32[128,4,96]{2,1,0:T(4,128)S(1)} all-gather(f32[32,4,96]{2,1,0:T(4,128)} %param.9), channel_id=1, replica_groups=mesh['ia'=16,'ja'=8,'ka'=4] {'ka'}, dimensions={0}, use_global_device_ids=true | all-gather | bytes 245760 | tf_op jit(solution)/shard_map/all_gather | solution.py:40
  30.1 22.2 %all_gather.6 = f32[128,4,96]{2,1,0:T(4,128)S(1)} all-gather(f32[16,4,96]{2,1,0:T(4,128)} %param.10), channel_id=1, replica_groups=mesh['ia'=16,'ja'=8,'ka'=4] {'ja'}, dimensions={0}, use_global_device_ids=true | all-gather | bytes 221184 | tf_op jit(solution)/shard_map/all_gather | solution.py:33
  52.7 1.3 dynamic-slice
  54.0 1.3 dynamic-slice.2
  55.9 5.5 %multiply_reduce_fusion = f32[384,32]{0,1:T(8,128)S(1)} fusion(f32[384,128]{0,1:T(8,128)S(1)} %copy.52, f32[32,128,128]{2,1,0:T(8,128)S(1)} %copy-done, f32[128,384,1]{0,1,2:T(8,128)S(1)} %bitcast.141), kind=kOutput, calls=%fused_computation | convolution fusion | flops 2419052544 | bytes 2539520 | tf_op jit(solution)/shard_map/dot_general | solution.py:34
  61.4 23.5 %all-reduce = f32[32,384]{1,0:T(8,128)S(1)} all-reduce(f32[32,384]{1,0:T(8,128)S(1)} %bitcast.142), channel_id=2, replica_groups=mesh['ia'=16,'ja'=8,'ka'=4] {'ja'}, use_global_device_ids=true, to_apply=%region_4.0.clone | all-reduce | flops 12288 | bytes 98304
  84.9 9.5 %all-reduce.1 = f32[4,384]{1,0:T(4,128)S(1)} all-reduce(f32[4,384]{1,0:T(4,128)S(1)} %constant_dynamic-slice_fusion), channel_id=3, replica_groups=mesh['ia'=16,'ja'=8,'ka'=4] {'ka'}, use_global_device_ids=true, to_apply=%region_5.0.clone | all-reduce | flops 1536 | bytes 12288
  94.5 0.7 dynamic-slice_reduce_fusion
  95.2 210.4 %all-reduce.5.cloned.1.call-done = (f32[4,96,96]{1,2,0:T(8,128)}, f32[4,96,96]{1,2,0:T(8,128)}) async-done(((f32[4,96,96]{1,2,0:T(8,128)}, f32[4,96,96]{1,2,0:T(8,128)}), (f32[4,96,96]{1,2,0:T(8,128)}, f32[4,96,96]{1,2,0:T(8,128)})) %all-reduce.5.cloned.1.call-update) | async-done | bytes 294928 | tf_op jit(solution)/shard_map/psum | solution.py:52
  305.6 1.0 fusion.24
  307.0 1.0 fusion.9
  308.0 8.8 %cholesky.107 = f32[96,96]{1,0:T(8,128)S(1)} custom-call(f32[96,96]{1,0:T(8,128)S(1)} %get-tuple-element.10), custom_call_target="Cholesky" | custom-call | tf_op jit(solution)/shard_map/jit(cholesky)/cholesky | solution.py:19
  316.8 0.6 compare_reduce_fusion
  317.5 0.7 fusion.5
  318.1 7.4 %custom-call.21 = f32[1,96,96]{1,2,0:T(8,128)S(1)} custom-call(f32[1,96,96]{2,1,0:T(8,128)S(1)} %fusion.5), custom_call_target="InvertDiagBlocksLowerTriangular" | custom-call | tf_op jit(solution)/shard_map/triangular_solve/custom-call.2 | solution.py:22
  325.6 0.2 fusion.11
  325.8 8.8 %cholesky.96 = f32[96,96]{1,0:T(8,128)S(1)} custom-call(f32[96,96]{1,0:T(8,128)S(1)} %get-tuple-element.11), custom_call_target="Cholesky" | custom-call | tf_op jit(solution)/shard_map/jit(cholesky)/cholesky | solution.py:19
  334.7 0.6 compare_reduce_fusion.1
  335.3 0.7 fusion.4
  336.0 7.4 %custom-call.19 = f32[1,96,96]{1,2,0:T(8,128)S(1)} custom-call(f32[1,96,96]{2,1,0:T(8,128)S(1)} %fusion.4), custom_call_target="InvertDiagBlocksLowerTriangular" | custom-call | tf_op jit(solution)/shard_map/triangular_solve/custom-call.2 | solution.py:22
  343.7 8.8 %cholesky.85 = f32[96,96]{1,0:T(8,128)S(1)} custom-call(f32[96,96]{1,0:T(8,128)S(1)} %get-tuple-element.12), custom_call_target="Cholesky" | custom-call | tf_op jit(solution)/shard_map/jit(cholesky)/cholesky | solution.py:19
  352.5 0.6 compare_reduce_fusion.2
  353.1 0.7 fusion.3
  353.8 7.4 %custom-call.17 = f32[1,96,96]{1,2,0:T(8,128)S(1)} custom-call(f32[1,96,96]{2,1,0:T(8,128)S(1)} %fusion.3), custom_call_target="InvertDiagBlocksLowerTriangular" | custom-call | tf_op jit(solution)/shard_map/triangular_solve/custom-call.2 | solution.py:22
  361.5 9.0 %cholesky.74 = f32[96,96]{1,0:T(8,128)S(1)} custom-call(f32[96,96]{1,0:T(8,128)S(1)} %get-tuple-element.9), custom_call_target="Cholesky" | custom-call | tf_op jit(solution)/shard_map/jit(cholesky)/cholesky | solution.py:19
  370.6 0.6 compare_reduce_fusion.3
  371.2 0.7 fusion.2
  371.9 7.4 %custom-call.15 = f32[1,96,96]{1,2,0:T(8,128)S(1)} custom-call(f32[1,96,96]{2,1,0:T(8,128)S(1)} %fusion.2), custom_call_target="InvertDiagBlocksLowerTriangular" | custom-call | tf_op jit(solution)/shard_map/triangular_solve/custom-call.2 | solution.py:22
  379.6 116.4 %psum.23 = f32[4,96]{1,0:T(4,128)S(1)} all-reduce(f32[4,96]{1,0:T(4,128)S(1)} %fusion.36), channel_id=1, replica_groups=mesh['ia'=16,'ja'=8,'ka'=4] {'ia','ja','ka'}, use_global_device_ids=true, to_apply=%region_6.10 | all-reduce | flops 384 | bytes 3072 | tf_op jit(solution)/shard_map/psum | solution.py:58
  496.0 0.6 divide_bitcast_fusion
  (25 shorter events, 2.2 us)
Async XLA Ops:
  7.2 48.7 %copy-start = (f32[32,128,128]{2,1,0:T(8,128)S(1)}, f32[32,128,128]{2,1,0:T(8,128)}, u32[]{:S(2)}) copy-start(f32[32,128,128]{2,1,0:T(8,128)} %param.8) | copy-start | bytes 6291460
  7.2 298.5 %all-reduce.5.cloned.1.call-start = ((), (), s32[]{:S(2)}) async-start(), calls=%async_computation | async-start | bytes 786432 | tf_op jit(solution)/shard_map/psum | solution.py:52
Sparse Core Ops, SparseCore 0:
  11.5 294.0 all-reduce.4
where the time goes:
time: 504 us; the launch traced here: 503 us
  waiting for transfers between devices  210 us (42%)
  blocking collectives  190 us (38%)
  other arithmetic  72.8 us (14%)
  between operations  14.9 us (3%)
  matrix products  11 us (2%)
    psum x1, waiting for transfers between devices, shards(): lax.psum((gram_of(factor_b), gram_of(factor_c)), ('ja', 'ka'))  210 us
    psum x1, blocking collectives, shards(): total = lax.psum(squares, ('ia', 'ja', 'ka'))  116 us
    another operation x12, other arithmetic, solve_normal(): factor_l = jnp.linalg.cholesky(normal_mat)  38.1 us
    unnamed x2, blocking collectives  33 us
    another operation x8, other arithmetic, solve_normal(): lax.linalg.triangular_solve(factor_l, lower_sol, left_side=True, lower=Tr...  32 us
    all_gather x1, blocking collectives, shards(): c_block = lax.all_gather(factor_c, 'ja', axis=0, tiled=True)  22.2 us
    all_gather x1, blocking collectives, shards(): piece = lax.all_gather(factor_b, 'ka', axis=0, tiled=True)  18.7 us
  transfers between devices with their start and end apart: 1, of which 1 were waited for; matrix products, arithmetic and copies ran while one was open for 2% of the time, Pallas kernels for 0%

commit v1 on v0

--- a/solution.py
+++ b/solution.py
@@ -37,7 +37,9 @@
         precision=highest,
         preferred_element_type=jnp.float32,
     ).reshape(rows_i, rows_j, width)
-    piece = lax.all_gather(factor_b, "ka", axis=0, tiled=True)
+    piece = jnp.concatenate(
+        lax.all_to_all(jnp.stack([factor_b] * lax.axis_size("ka")), "ka", 0, 0), axis=0
+    )
     gram_sum = jnp.zeros((starts, col_count, col_count), jnp.float32)
     count = piece.shape[0]
     flat_rows = piece.reshape(count, width)

time: 504 us -> 549 us (1.089)
  waiting for transfers between devices: 210 us -> 256 us
  blocking collectives: 190 us -> 177 us
  starting transfers between devices: 0.04 us -> 10.9 us
    psum x1, waiting for transfers between devices: 210 us -> 256 us  [shards(): lax.psum((gram_of(factor_b), gram_of(factor_c)), ('ja', 'ka'))]
    all_gather x1 -> x0, blocking collectives: 18.7 us -> none  [shards(): piece = lax.all_gather(factor_b, 'ka', axis=0, tiled=True)]
    all_to_all x0 -> x1, starting transfers between devices: none -> 10.8 us  [shards(): lax.all_to_all(jnp.stack([factor_b] * lax.axis_size('ka')), 'ka', 0, 0)]
    psum x1, blocking collectives: 116 us -> 125 us  [shards(): total = lax.psum(squares, ('ia', 'ja', 'ka'))]
  transfers between devices with their start and end apart: 1 -> 2, of which waited for: 1 -> 1; matrix products, arithmetic and copies ran while one was open for 2% -> 4% of each run, Pallas kernels for 0% -> 0%
where the time goes in v1:
time: 549 us; the launch traced here: 548 us
  waiting for transfers between devices  256 us (47%)
  blocking collectives  177 us (32%)
  other arithmetic  72.6 us (13%)
  between operations  14.9 us (3%)
  matrix products  11 us (2%)
  starting transfers between devices  10.9 us (2%)
  local copies, waits for them, and re-layouts  5.5 us (1%)
    psum x1, waiting for transfers between devices, shards(): lax.psum((gram_of(factor_b), gram_of(factor_c)), ('ja', 'ka'))  256 us
    psum x1, blocking collectives, shards(): total = lax.psum(squares, ('ia', 'ja', 'ka'))  125 us
    another operation x12, other arithmetic, solve_normal(): factor_l = jnp.linalg.cholesky(normal_mat)  37.9 us
    another operation x8, other arithmetic, solve_normal(): lax.linalg.triangular_solve(factor_l, lower_sol, left_side=True, lower=Tr...  32 us
    unnamed x2, blocking collectives  30 us
    all_gather x1, blocking collectives, shards(): c_block = lax.all_gather(factor_c, 'ja', axis=0, tiled=True)  21.9 us
  transfers between devices with their start and end apart: 2, of which 1 were waited for; matrix products, arithmetic and copies ran while one was open for 4% of the time, Pallas kernels for 0%

profile of v1, /device:TPU:1, one launch (start us, length us, event | category | flops | bytes accessed | tf_op | source)
XLA Modules:
  0.0 548.2 jit_solution(10203331546459965260)
XLA Ops:
  7.2 2.1 fusion.22
  9.3 2.1 fusion
  11.4 1.6 stack.18
  13.0 10.8 %all-to-all-start = ((f32[4,32,4,96]{3,2,1,0:T(4,128)}), f32[4,32,4,96]{3,2,1,0:T(4,128)S(1)}, u32[]{:S(2)}, u32[]{:S(2)}) async-start(f32[4,32,4,96]{3,2,1,0:T(4,128)} %stack.18), calls=%async_computation | async-start | bytes 524288 | tf_op jit(solution)/shard_map/all_to_all | solution.py:41
  23.8 21.9 %all_gather.3 = f32[128,4,96]{2,1,0:T(4,128)S(1)} all-gather(f32[16,4,96]{2,1,0:T(4,128)} %param.10), channel_id=1, replica_groups=mesh['ia'=16,'ja'=8,'ka'=4] {'ja'}, dimensions={0}, use_global_device_ids=true | all-gather | bytes 221184 | tf_op jit(solution)/shard_map/all_gather | solution.py:33
  45.9 1.3 dynamic-slice
  47.1 1.3 dynamic-slice.2
  49.1 256.5 %all-reduce.5.cloned.1.call-done = (f32[4,96,96]{1,2,0:T(8,128)}, f32[4,96,96]{1,2,0:T(8,128)}) async-done(((f32[4,96,96]{1,2,0:T(8,128)}, f32[4,96,96]{1,2,0:T(8,128)}), (f32[4,96,96]{1,2,0:T(8,128)}, f32[4,96,96]{1,2,0:T(8,128)})) %all-reduce.5.cloned.1.call-update) | async-done | bytes 294928 | tf_op jit(solution)/shard_map/psum | solution.py:54
  305.5 1.0 fusion.24
  306.9 1.0 fusion.9
  307.9 8.8 %cholesky.107 = f32[96,96]{1,0:T(8,128)S(1)} custom-call(f32[96,96]{1,0:T(8,128)S(1)} %get-tuple-element.10), custom_call_target="Cholesky" | custom-call | tf_op jit(solution)/shard_map/jit(cholesky)/cholesky | solution.py:19
  316.7 0.6 compare_reduce_fusion
  317.4 0.7 fusion.5
  318.0 7.4 %custom-call.21 = f32[1,96,96]{1,2,0:T(8,128)S(1)} custom-call(f32[1,96,96]{2,1,0:T(8,128)S(1)} %fusion.5), custom_call_target="InvertDiagBlocksLowerTriangular" | custom-call | tf_op jit(solution)/shard_map/triangular_solve/custom-call.2 | solution.py:22
  325.6 5.5 %multiply_reduce_fusion = f32[384,32]{0,1:T(8,128)S(1)} fusion(f32[384,128]{0,1:T(8,128)S(1)} %bitcast.138, f32[32,128,128]{2,1,0:T(8,128)S(1)} %copy-done, f32[128,384,1]{0,1,2:T(8,128)S(1)} %bitcast.137), kind=kOutput, calls=%fused_computation | convolution fusion | flops 2419052544 | bytes 2539520 | tf_op jit(solution)/shard_map/dot_general | solution.py:34
  331.1 20.5 %all-reduce = f32[32,384]{1,0:T(8,128)S(1)} all-reduce(f32[32,384]{1,0:T(8,128)S(1)} %bitcast.139), channel_id=2, replica_groups=mesh['ia'=16,'ja'=8,'ka'=4] {'ja'}, use_global_device_ids=true, to_apply=%region_4.0.clone | all-reduce | flops 12288 | bytes 98304
  351.6 9.5 %all-reduce.1 = f32[4,384]{1,0:T(4,128)S(1)} all-reduce(f32[4,384]{1,0:T(4,128)S(1)} %constant_dynamic-slice_fusion), channel_id=3, replica_groups=mesh['ia'=16,'ja'=8,'ka'=4] {'ka'}, use_global_device_ids=true, to_apply=%region_5.0.clone | all-reduce | flops 1536 | bytes 12288
  361.1 0.7 dynamic-slice_reduce_fusion
  362.2 8.8 %cholesky.96 = f32[96,96]{1,0:T(8,128)S(1)} custom-call(f32[96,96]{1,0:T(8,128)S(1)} %get-tuple-element.11), custom_call_target="Cholesky" | custom-call | tf_op jit(solution)/shard_map/jit(cholesky)/cholesky | solution.py:19
  371.0 0.6 compare_reduce_fusion.1
  371.7 0.7 fusion.4
  372.3 7.4 %custom-call.19 = f32[1,96,96]{1,2,0:T(8,128)S(1)} custom-call(f32[1,96,96]{2,1,0:T(8,128)S(1)} %fusion.4), custom_call_target="InvertDiagBlocksLowerTriangular" | custom-call | tf_op jit(solution)/shard_map/triangular_solve/custom-call.2 | solution.py:22
  380.0 8.8 %cholesky.85 = f32[96,96]{1,0:T(8,128)S(1)} custom-call(f32[96,96]{1,0:T(8,128)S(1)} %get-tuple-element.12), custom_call_target="Cholesky" | custom-call | tf_op jit(solution)/shard_map/jit(cholesky)/cholesky | solution.py:19
  388.9 0.6 compare_reduce_fusion.2
  389.5 0.7 fusion.3
  390.2 7.4 %custom-call.17 = f32[1,96,96]{1,2,0:T(8,128)S(1)} custom-call(f32[1,96,96]{2,1,0:T(8,128)S(1)} %fusion.3), custom_call_target="InvertDiagBlocksLowerTriangular" | custom-call | tf_op jit(solution)/shard_map/triangular_solve/custom-call.2 | solution.py:22
  397.9 8.8 %cholesky.74 = f32[96,96]{1,0:T(8,128)S(1)} custom-call(f32[96,96]{1,0:T(8,128)S(1)} %get-tuple-element.9), custom_call_target="Cholesky" | custom-call | tf_op jit(solution)/shard_map/jit(cholesky)/cholesky | solution.py:19
  406.7 0.6 compare_reduce_fusion.3
  407.4 0.7 fusion.2
  408.0 7.4 %custom-call.15 = f32[1,96,96]{1,2,0:T(8,128)S(1)} custom-call(f32[1,96,96]{2,1,0:T(8,128)S(1)} %fusion.2), custom_call_target="InvertDiagBlocksLowerTriangular" | custom-call | tf_op jit(solution)/shard_map/triangular_solve/custom-call.2 | solution.py:22
  415.8 125.0 %psum.23 = f32[4,96]{1,0:T(4,128)S(1)} all-reduce(f32[4,96]{1,0:T(4,128)S(1)} %fusion.36), channel_id=1, replica_groups=mesh['ia'=16,'ja'=8,'ka'=4] {'ia','ja','ka'}, use_global_device_ids=true, to_apply=%region_6.10 | all-reduce | flops 384 | bytes 3072 | tf_op jit(solution)/shard_map/psum | solution.py:60
  540.8 0.6 divide_bitcast_fusion
  (26 shorter events, 2.2 us)
Async XLA Ops:
  7.2 318.4 %copy-start = (f32[32,128,128]{2,1,0:T(8,128)S(1)}, f32[32,128,128]{2,1,0:T(8,128)}, u32[]{:S(2)}) copy-start(f32[32,128,128]{2,1,0:T(8,128)} %param.8) | copy-start | bytes 6291460
  7.2 298.4 %all-reduce.5.cloned.1.call-start = ((), (), s32[]{:S(2)}) async-start(), calls=%async_computation.1 | async-start | bytes 786432 | tf_op jit(solution)/shard_map/psum | solution.py:54
  13.0 312.4 %all-to-all-start = ((f32[4,32,4,96]{3,2,1,0:T(4,128)}), f32[4,32,4,96]{3,2,1,0:T(4,128)S(1)}, u32[]{:S(2)}, u32[]{:S(2)}) async-start(f32[4,32,4,96]{3,2,1,0:T(4,128)} %stack.18), calls=%async_computation | async-start | bytes 524288 | tf_op jit(solution)/shard_map/all_to_all | solution.py:41
Sparse Core Ops, SparseCore 0:
  11.5 293.9 all-reduce.4
